TPU v7x, 32 devices: a whole 2x2x4 slice. The times are simulated.
32 devices in a mesh: tile: 8 (over z, y), lev: 4 (over x, core).
Axes of the slice: x: 2, y: 2, z: 4, core: 2. Of those that a mesh axis runs over, the one named last changes fastest.
Arguments:
- cotangent: bfloat16 [3072, 128, 128], P('lev', 'tile'), may hold values from -6 to 6
- mix_weight: bfloat16 [3072, 3072], P(None, 'tile'), may hold values from -0.109375 to 0.109375
- kernel: float32 [3072, 9], P('lev'), may hold values from -2 to 2
- send_rows: int32 [8, 8, 41], P('tile'), may hold values from -1 to 291, as said below
- recv_cells: int32 [8, 8, 41], P('tile'), may hold values from -1 to 1918, as said below
- recv_weight: float32 [8, 4, 8, 41], P('tile'), may hold values from 0 to 1, as said below
Outputs:
- grad_input: bfloat16 [3072, 128, 128], P('lev', 'tile')
Inputs may be any that keep to these rules, and one draw needn't show every extreme that they name: `send_rows`: partner d is always a strip of the other panel. Every slot of the side columns (with the four corners) of strip s appears exactly once over all d and k, the slots of row 0 only for the strip at place 0 of a panel and those of row 17 only for the strip at place 4 - 1; no other slots appear. Used entries of a block come first, and some pair uses all 41. recv_cells[d, s, k] is -1 exactly where send_rows[s, d, k] is -1; otherwise its row is at most 14 and its column at most 126, so all four corners lie in strip d; the largest cell is reached. `recv_weight`: the four weights of an entry are the bilinear weights of a point in the donor cell and sum to one.
All inputs are finite; a program needn't handle non-finite values.
Results may differ from a plain program's by a relative error of at most 0.0049.
Values may be sent and summed in bfloat16 or wider, within the bound.
A program may use at most 128 MiB of HBM per device.

v0:
```python
import jax
import jax.numpy as jnp
from jax import lax
from jax.sharding import PartitionSpec as P


def padded_2(cells, sides, width):
    for axis, dim in sides:
        count = lax.axis_size(axis)
        head = lax.slice_in_dim(cells, 0, width, axis=dim)
        tail = lax.slice_in_dim(cells, cells.shape[dim] - width, cells.shape[dim], axis=dim)
        cells = jnp.concatenate(
            [
                lax.ppermute(tail, axis, [(i, (i + 1) % count) for i in range(count)]),
                cells,
                lax.ppermute(head, axis, [((i + 1) % count, i) for i in range(count)]),
            ],
            axis=dim,
        )
    return cells


def stencil_adjoint(grad_block, kernel):
    feat_local, tile_rows, tile_cols = grad_block.shape
    padded = jnp.pad(grad_block.astype(jnp.float32), ((0, 0), (2, 2), (2, 2)))
    summed = jnp.zeros((feat_local, tile_rows + 2, tile_cols + 2), jnp.float32)
    for row_shift in (-1, 0, 1):
        for col_shift in (-1, 0, 1):
            kernel_tap = kernel[:, 3 * (row_shift + 1) + col_shift + 1]
            window_part = padded[
                :,
                1 - row_shift : 3 - row_shift + tile_rows,
                1 - col_shift : 3 - col_shift + tile_cols,
            ]
            summed = summed + kernel_tap[:, None, None] * window_part
    return summed


def cycle_of(extended):
    return jnp.concatenate(
        [extended[:, 0, :], extended[:, -1, :], extended[:, 1:-1, 0], extended[:, 1:-1, -1]], axis=1
    )


def deposit(running, values, cell_index, weight_rows, row_length):
    is_used = cell_index >= 0
    base_cell = jnp.maximum(cell_index, 0)
    spread = values.astype(jnp.float32)
    for corner, offset in enumerate((0, 1, row_length, row_length + 1)):
        running = running.at[:, base_cell + offset].add(
            spread * jnp.where(is_used, weight_rows[corner], 0.0)[None, :]
        )
    return running


def per_device(cotangent, mix_weight, kernel, send_rows, recv_cells, recv_weight):
    feat_local, tile_rows, tile_cols = cotangent.shape
    cell_count = tile_rows * tile_cols
    flat_grad = cotangent.reshape(feat_local, cell_count)
    level_index = lax.axis_index("lev")
    own_rows = lax.dynamic_slice_in_dim(mix_weight, level_index * feat_local, feat_local, 0)
    weight_rows = lax.all_gather(own_rows, "tile", axis=1, tiled=True)
    grad_mix = jnp.dot(
        weight_rows,
        lax.all_gather(flat_grad, "lev", axis=0, tiled=True),
        preferred_element_type=jnp.float32,
    ).astype(jnp.bfloat16)
    extended = stencil_adjoint(grad_mix.reshape(feat_local, tile_rows, tile_cols), kernel)
    cycle_values = cycle_of(extended).astype(jnp.bfloat16)
    tile_count = lax.axis_size("tile")
    strip_count = tile_count // 2
    tile_here = lax.axis_index("tile")
    place_index = (tile_here + strip_count // 2) % tile_count % strip_count
    keep_top = (place_index != 0).astype(jnp.float32)
    keep_bottom = (place_index != strip_count - 1).astype(jnp.float32)
    edge_rows = jnp.stack(
        [extended[:, 0, 1:-1] * keep_top, extended[:, -1, 1:-1] * keep_bottom], axis=1
    )
    bordered = padded_2(edge_rows.astype(jnp.bfloat16), (("tile", 1),), 1).astype(edge_rows.dtype)
    interior = extended[:, 1:-1, 1:-1]
    interior = interior.at[:, 0, :].add(bordered[:, 0, :]).at[:, -1, :].add(bordered[:, 3, :])
    running = interior.reshape(feat_local, cell_count)
    cell_lists = recv_cells[0]
    weight_lists = recv_weight[0]
    slot_lists = lax.all_to_all(send_rows[0], "tile", split_axis=0, concat_axis=0, tiled=True)
    cycle_size = cycle_values.shape[1]
    shard_piece = lax.all_gather(cycle_values, "tile", axis=1, tiled=True)
    sources = shard_piece.shape[1] // cycle_size
    local_slots = (
        jnp.arange(sources, dtype=jnp.int32)[:, None] * cycle_size + jnp.maximum(slot_lists, 0)
    ).reshape(-1)
    values = jnp.take(shard_piece, local_slots, axis=1)
    cells_part = cell_lists.reshape(-1)
    weights_part = weight_lists.reshape(4, -1)
    running = deposit(running, values, cells_part, weights_part, tile_cols)
    return running.reshape(feat_local, tile_rows, tile_cols).astype(jnp.bfloat16)


def solution(mesh):
    in_specs = (
        P("lev", "tile", None),
        P(None, "tile"),
        P("lev", None),
        P("tile", None, None),
        P("tile", None, None),
        P("tile", None, None, None),
    )
    out_specs = P("lev", "tile", None)
    return jax.shard_map(
        per_device, mesh=mesh, in_specs=in_specs, out_specs=out_specs, check_vma=False
    )
```

profile of v0, /device:TPU:17, one launch (start us, length us, event | category | flops | bytes accessed | tf_op | source)
XLA Modules:
  0.0 360.1 jit_solution(4709097112009996498)
XLA Ops:
  6.5 0.0 copy-start
  6.5 0.0 copy-start.4
  6.5 0.0 all-gather.5.cloned.1.call-start
  6.5 1.7 copy-done
  8.2 0.9 constant_dynamic-slice_fusion
  9.1 0.0 all-gather.5.cloned.1.call-update
  9.1 0.0 all-gather.7.cloned.1.call-start
  9.1 4.9 %copy.22 = bf16[96,8,16,128]{3,1,2,0:T(8,128)(2,1)} copy(bf16[96,8,16,128]{3,2,1,0:T(8,128)(2,1)} %bitcast.36) | data formatting | bytes 6291456
  14.0 0.0 all-gather.7.cloned.1.call-update
  14.0 0.0 all-gather.9.cloned.1.call-start
  14.1 0.0 copy-done.4
  14.1 0.1 slice_reduce_fusion.8
  14.2 76.1 %all-gather.5.cloned.1.call-done = bf16[768,3072]{1,0:T(8,128)(2,1)} async-done(((bf16[768,384]{1,0:T(8,128)(2,1)}), bf16[768,3072]{1,0:T(8,128)(2,1)}) %all-gather.5.cloned.1.call-update) | async-done | bytes 4718608 | tf_op jit(solution)/shard_map/all_gather | solution.py:62
  90.2 83.6 %all-gather.7.cloned.1.call-done = bf16[3072,2048]{1,0:T(8,128)(2,1)} async-done(((bf16[768,2048]{1,0:T(8,128)(2,1)}), bf16[3072,2048]{1,0:T(8,128)(2,1)}) %all-gather.7.cloned.1.call-update) | async-done | bytes 12582928 | tf_op jit(solution)/shard_map/all_gather | solution.py:65
  173.8 15.4 %convolution_convert_fusion = bf16[768,2048]{1,0:T(8,128)(2,1)} fusion(bf16[768,3072]{1,0:T(8,128)(2,1)} %all-gather.5.cloned.1.call-done, bf16[3072,2048]{1,0:T(8,128)(2,1)} %all-gather.7.cloned.1.call-done), kind=kOutput, calls=%fused_computation.23 | convolution fusion | flops 9665249280 | bytes 20447232 | tf_op jit(solution)/shard_map/dot_general | solution.py:63
  189.2 4.7 %copy.15 = bf16[768,2048]{0,1:T(8,128)(2,1)} copy(bf16[768,2048]{1,0:T(8,128)(2,1)} %convolution_convert_fusion) | data formatting | bytes 6291456 | tf_op jit(solution)/shard_map/convert_element_type | solution.py:25
  193.9 5.8 %pad_convert_fusion = f32[768,20,132]{0,2,1:T(8,128)} fusion(bf16[768,16,128]{0,2,1:T(8,128)(2,1)} %bitcast.34), kind=kLoop, calls=%fused_computation.22 | loop fusion | flops 2027520 | bytes 11255808 | tf_op jit(solution)/shard_map/jit(_pad)/pad | solution.py:25
  199.7 0.0 copy-start.2
  199.7 0.0 copy-start.3
  199.7 28.3 %fusion.25 = (bf16[768,18,130]{0,2,1:T(8,128)(2,1)}, f32[768,18,130]{0,2,1:T(8,128)}) fusion(f32[768,20,132]{0,2,1:T(8,128)} %pad_convert_fusion, f32[768]{0:T(1024)S(1)} %get-tuple-element.36, f32[768]{0:T(1024)S(1)} %get-tuple-element.37, f32[768]{0:T(1024)S(1)} %get-tuple-element.30, f32[768]{0:T(1024)S(1)} %get-tuple-element.31, ...), kind=kLoop, calls=%fused_computation.90 | loop fusion | flops 32348160 | bytes 75506688 | tf_op jit(solution)/shard_map/convert.14
  228.0 1.1 fusion.27
  229.1 1.1 slice_bitcast_fusion.1
  230.2 0.8 maximum_bitcast_fusion
  231.0 0.0 all-gather.9.cloned.1.call-update
  231.0 5.5 %all-to-all-start = ((s32[8,1,41]{2,1,0:T(1,128)}), s32[8,1,41]{2,1,0:T(1,128)S(1)}, u32[]{:S(2)}, u32[]{:S(2)}) async-start(s32[8,1,41]{2,1,0:T(1,128)} %bitcast.2), calls=%async_computation | async-start | bytes 8192 | tf_op jit(solution)/shard_map/all_to_all | solution.py:85
  236.5 0.0 copy-done.2
  236.5 0.1 squeeze.37
  236.6 0.1 squeeze.38
  236.7 0.1 squeeze.39
  236.8 0.1 squeeze.40
  236.9 0.0 copy-done.3
  236.9 0.1 ge.30
  237.0 0.1 reshape.278
  237.1 0.1 reshape.280
  237.1 0.1 reshape.282
  237.2 0.1 reshape.284
  237.3 0.1 reshape.286
  237.4 0.1 reshape.288
  237.6 0.1 add.204
  237.7 0.1 add.209
  237.7 0.1 add.205
  237.8 0.1 reshape.246
  237.9 1.8 all-to-all-done
  239.7 0.1 max.55
  239.8 0.1 max.53
  239.9 1.3 fusion.19
  241.2 0.3 collective-permute-start
  241.5 2.1 collective-permute-start.1
  243.7 6.3 %slice.198 = f32[768,16,128]{0,2,1:T(8,128)} slice(f32[768,18,130]{0,2,1:T(8,128)} %get-tuple-element.39), slice={[0:768], [1:17], [1:129]} | slice | bytes 12582912 | tf_op jit(solution)/shard_map/slice | solution.py:80
  250.0 6.7 %collective-permute-done = bf16[768,1,128]{0,2,1:T(8,128)(2,1)S(1)} collective-permute-done((bf16[768,1,128]{0,2,1:T(8,128)(2,1)S(1)}, bf16[768,1,128]{0,2,1:T(8,128)(2,1)S(1)}, u32[]{:S(2)}, u32[]{:S(2)}) %collective-permute-start) | collective-permute-done | bytes 196640 | tf_op jit(solution)/shard_map/ppermute | solution.py:14
  256.7 0.0 collective-permute-done.1
  256.7 1.8 fusion.17
  258.5 1.8 fusion.16
  260.3 40.2 %all-gather.9.cloned.1.call-done = bf16[8,292,768]{2,1,0:T(8,128)(2,1)} async-done(((bf16[1,292,768]{2,1,0:T(8,128)(2,1)}), bf16[8,292,768]{2,1,0:T(8,128)(2,1)}) %all-gather.9.cloned.1.call-update) | async-done | bytes 3588112 | tf_op jit(solution)/shard_map/all_gather | solution.py:87
  300.4 4.7 %reshape.290 = bf16[2336,768]{1,0:T(8,128)(2,1)} reshape(bf16[8,292,768]{2,1,0:T(8,128)(2,1)} %all-gather.9.cloned.1.call-done) | data formatting | bytes 7176192
  305.2 5.0 %gather_fusion = bf16[328,768]{1,0:T(8,128)(2,1)S(1)} fusion(bf16[768,2336]{0,1:T(8,128)(2,1)} %bitcast.32, s32[1024]{0:T(1024)S(1)} %pad_clamp_fusion), kind=kCustom, calls=%fused_computation | custom fusion | bytes 1008928 | tf_op jit(solution)/shard_map/jit(_take)/gather | solution.py:92
  310.1 8.4 %scatter_custom_fusion = f32[768,2048]{0,1:T(8,128)} fusion(f32[768,2048]{0,1:T(8,128)} %bitcast.1, s32[328]{0:T(512)S(1)} %reshape.246, f32[328]{0:T(512)S(1)} %get-tuple-element.62, bf16[328,768]{1,0:T(8,128)(2,1)S(1)} %gather_fusion, pred[328]{0:T(512)(128)(4,1)S(1)} %compare_and_fusion), kind=kCustom, calls=%fused_computation.30 | custom fusion | flops 1007616 | bytes 6797824 | tf_op jit(solution)/shard_map/scatter-add | solution.py:50
  318.5 8.4 %scatter_custom_fusion.1 = f32[768,2048]{0,1:T(8,128)} fusion(f32[768,2048]{0,1:T(8,128)} %scatter_custom_fusion, s32[328]{0:T(512)S(1)} %fusion.21, f32[328]{0:T(512)S(1)} %get-tuple-element.61, bf16[328,768]{1,0:T(8,128)(2,1)S(1)} %gather_fusion, pred[328]{0:T(512)(128)(4,1)S(1)} %compare_and_fusion), kind=kCustom, calls=%fused_computation.31 | custom fusion | flops 1007616 | bytes 6797824 | tf_op jit(solution)/shard_map/scatter-add | solution.py:50
  326.9 8.4 %scatter_custom_fusion.2 = f32[768,2048]{0,1:T(8,128)} fusion(f32[768,2048]{0,1:T(8,128)} %scatter_custom_fusion.1, s32[328]{0:T(512)S(1)} %fusion.22, f32[328]{0:T(512)S(1)} %get-tuple-element.60, bf16[328,768]{1,0:T(8,128)(2,1)S(1)} %gather_fusion, pred[328]{0:T(512)(128)(4,1)S(1)} %compare_and_fusion), kind=kCustom, calls=%fused_computation.32 | custom fusion | flops 1007616 | bytes 6797824 | tf_op jit(solution)/shard_map/scatter-add | solution.py:50
  335.3 0.0 copy-start.1
  335.3 8.5 %scatter_custom_fusion.3 = f32[768,2048]{0,1:T(8,128)} fusion(f32[768,2048]{0,1:T(8,128)} %scatter_custom_fusion.2, s32[328]{0:T(512)S(1)} %fusion.23, f32[328]{0:T(512)S(1)} %get-tuple-element.59, bf16[328,768]{1,0:T(8,128)(2,1)S(1)} %gather_fusion, pred[328]{0:T(512)(128)(4,1)S(1)} %compare_and_fusion), kind=kCustom, calls=%fused_computation.29 | custom fusion | flops 1007616 | bytes 6797824 | tf_op jit(solution)/shard_map/scatter-add | solution.py:50
  343.8 4.8 %convert_element_type.35 = bf16[768,2048]{0,1:T(8,128)(2,1)} convert(f32[768,2048]{0,1:T(8,128)} %scatter_custom_fusion.3) | non-fusion elementwise | flops 1572864 | bytes 9437184 | tf_op jit(solution)/shard_map/convert_element_type | solution.py:96
  348.6 5.0 %copy.14 = bf16[768,16,128]{2,1,0:T(8,128)(2,1)} copy(bf16[768,16,128]{0,2,1:T(8,128)(2,1)} %bitcast.35) | data formatting | bytes 6291456 | tf_op jit(solution)/shard_map/convert_element_type | solution.py:96
  353.5 0.0 copy-done.1
  (13 shorter events, 0.2 us)
Async XLA Ops:
  6.5 1.7 copy-start
  6.5 7.5 %copy-start.4 = (f32[768,9]{0,1:T(8,128)S(1)}, f32[768,9]{0,1:T(8,128)}, u32[]{:S(2)}) copy-start(f32[768,9]{0,1:T(8,128)} %param.12) | copy-start | bytes 82948
  6.5 83.7 %all-gather.5.cloned.1.call-start = ((), (), s32[]{:S(2)}) async-start(), calls=%async_computation.1 | async-start | bytes 5308416 | tf_op jit(solution)/shard_map/all_gather | solution.py:62
  9.1 164.7 %all-gather.7.cloned.1.call-start = ((), (), s32[]{:S(2)}) async-start(), calls=%async_computation.2 | async-start | bytes 15728640 | tf_op jit(solution)/shard_map/all_gather | solution.py:65
  14.0 286.4 %all-gather.9.cloned.1.call-start = ((), (), s32[]{:S(2)}) async-start(), calls=%async_computation.3 | async-start | bytes 4091904 | tf_op jit(solution)/shard_map/all_gather | solution.py:87
  199.7 36.8 %copy-start.2 = (f32[1,4,8,41]{3,2,1,0:T(8,128)S(1)}, f32[1,4,8,41]{3,2,1,0:T(8,128)}, u32[]{:S(2)}) copy-start(f32[1,4,8,41]{3,2,1,0:T(8,128)} %param.15) | copy-start | bytes 15748
  199.7 37.1 %copy-start.3 = (s32[1,8,41]{2,1,0:T(8,128)S(1)}, s32[1,8,41]{2,1,0:T(8,128)}, u32[]{:S(2)}) copy-start(s32[1,8,41]{2,1,0:T(8,128)} %param.14) | copy-start | bytes 3940
  231.0 8.6 %all-to-all-start = ((s32[8,1,41]{2,1,0:T(1,128)}), s32[8,1,41]{2,1,0:T(1,128)S(1)}, u32[]{:S(2)}, u32[]{:S(2)}) async-start(s32[8,1,41]{2,1,0:T(1,128)} %bitcast.2), calls=%async_computation | async-start | bytes 8192 | tf_op jit(solution)/shard_map/all_to_all | solution.py:85
  241.2 15.5 %collective-permute-start = (bf16[768,1,128]{0,2,1:T(8,128)(2,1)S(1)}, bf16[768,1,128]{0,2,1:T(8,128)(2,1)S(1)}, u32[]{:S(2)}, u32[]{:S(2)}) collective-permute-start(bf16[768,1,128]{0,2,1:T(8,128)(2,1)S(1)} %get-tuple-element.40), channel_id=1, source_target_pairs={{0,4},{4,8},{8,12},{12,16},{16,20},{20,24},{24,28},{28,0},{1,5},{5... | collective-permute-start | bytes 589832 | tf_op jit(solution)/shard_map/ppermute | solution.py:14
  241.5 15.2 %collective-permute-start.1 = (bf16[768,1,128]{0,2,1:T(8,128)(2,1)S(1)}, bf16[768,1,128]{0,2,1:T(8,128)(2,1)S(1)}, u32[]{:S(2)}, u32[]{:S(2)}) collective-permute-start(bf16[768,1,128]{0,2,1:T(8,128)(2,1)S(1)} %get-tuple-element.41), channel_id=1, source_target_pairs={{4,0},{8,4},{12,8},{16,12},{20,16},{24,20},{28,24},{0,28},{5,1},{9... | collective-permute-start | bytes 589832 | tf_op jit(solution)/shard_map/ppermute | solution.py:16
  335.3 18.3 %copy-start.1 = (bf16[3072,384]{1,0:T(8,128)(2,1)S(1)}, bf16[3072,384]{1,0:T(8,128)(2,1)}, u32[]{:S(2)}) copy-start(bf16[3072,384]{1,0:T(8,128)(2,1)} %param.11) | copy-start | bytes 7077892
Sparse Core Ops, SparseCore 0:
  9.4 80.7 all-gather.4
  91.8 82.0 all-gather.6
  231.2 69.2 all-gather.8
where the time goes:
time: 364 us; the launch traced here: 360 us
  waiting for transfers between devices  208 us (57%)
  other arithmetic  78.4 us (22%)
  local copies, waits for them, and re-layouts  36.6 us (10%)
  matrix products  15.4 us (4%)
  between operations  13.3 us (4%)
  starting transfers between devices  7.99 us (2%)
    all_gather x1, waiting for transfers between devices, per_device(): lax.all_gather(flat_grad, 'lev', axis=0, tiled=True)  83.6 us
    all_gather x1, waiting for transfers between devices, per_device(): weight_rows = lax.all_gather(own_rows, 'tile', axis=1, tiled=True)  76.1 us
    all_gather x1, waiting for transfers between devices, per_device(): shard_piece = lax.all_gather(cycle_values, 'tile', axis=1, tiled=True)  40.2 us
    scatter-add x4, other arithmetic, deposit(): running.at[:, base_cell + offset]  33.7 us
    another operation x1, other arithmetic  28.3 us
    dot_general x1, matrix products, per_device(): jnp.dot(weight_rows, lax.all_gather(flat_grad, 'lev', axis=0, tiled=True)...  15.4 us
    unnamed x13, local copies, waits for them, and re-layouts  11.3 us
  transfers between devices with their start and end apart: 6, of which 5 were waited for; matrix products, arithmetic and copies ran while one was open for 5% of the time, Pallas kernels for 0%

commit v1 on v0

v1 whole, which is shorter than its diff:
```python
import functools

import jax
import jax.numpy as jnp
from jax import lax
from jax.experimental import pallas as pl
from jax.experimental.pallas import tpu as pltpu
from jax.sharding import PartitionSpec as P

MESH = pl.DeviceIdType.MESH


def mix_kernel(n_tile, n_lev, chunks, c_ref, w_ref, g_ref, wg, cg, local_sem, ws, wr, cs, cr):
    t = lax.axis_index("tile")
    l = lax.axis_index("lev")
    feat, cells = c_ref.shape
    cb = w_ref.shape[1]
    half_t, half_l = n_tile // 2, n_lev // 2
    width = cells // chunks
    per = feat // cb
    joined = len(wg.shape) == 3 and wg.shape[0] == n_lev and wg.shape[2] == feat
    t_mate = t + 1 - 2 * lax.rem(t, 2)
    l_mate = l + 1 - 2 * lax.rem(l, 2)

    def t_of(base, k):
        return lax.rem(base + 2 * k + 2 * n_tile, n_tile)

    def l_of(base, k):
        return lax.rem(base + 2 * k + 2 * n_lev, n_lev)

    barrier = pltpu.get_barrier_semaphore()
    peers = [(t_of(t, k), l) for k in range(1, half_t)] + [(t_mate, l), (t, l_mate)]
    peers += [(t, l_of(l, k)) for k in range(1, half_l)]
    for peer in peers:
        pl.semaphore_signal(barrier, inc=1, device_id=peer, device_id_type=MESH)
    pl.semaphore_wait(barrier, len(peers))

    def w_slot(index):
        if joined:
            return wg.at[index // per, :, pl.ds(pl.multiple_of(lax.rem(index, per) * cb, cb), cb)]
        return wg.at[index]

    own_w = w_ref.at[pl.ds(pl.multiple_of(l * feat, feat), feat)]

    def w_copy(lane, k, index, source, to):
        return pltpu.make_async_remote_copy(
            src_ref=source, dst_ref=w_slot(index), send_sem=ws.at[lane, k], recv_sem=wr.at[lane, k],
            device_id=(to, l), device_id_type=MESH)

    def c_piece(ref, ch):
        return ref.at[:, ch * width:(ch + 1) * width]

    def c_copy(lane, k, ch, index, source, to):
        return pltpu.make_async_remote_copy(
            src_ref=source, dst_ref=c_piece(cg.at[index], ch), send_sem=cs.at[lane, k, ch],
            recv_sem=cr.at[lane, k, ch], device_id=(t, to), device_id_type=MESH)

    sends = []

    def start(copy):
        copy.start()
        sends.append(copy)

    for ch in range(chunks):
        for k in range(1, half_l):
            start(c_copy(0, k, ch, l, c_piece(c_ref, ch), l_of(l, k)))
    for k in range(1, half_t):
        start(w_copy(0, k, t, own_w, t_of(t, k)))
    start(w_copy(1, 0, t, own_w, t_mate))
    for ch in range(chunks):
        start(c_copy(1, 0, ch, l, c_piece(c_ref, ch), l_mate))
    keep_w = pltpu.make_async_copy(own_w, w_slot(t), local_sem.at[0])
    keep_c = pltpu.make_async_copy(c_ref, cg.at[l], local_sem.at[1])
    keep_w.start()
    keep_c.start()

    def pass_w(k):
        index = t_of(t, -k)
        w_copy(0, k, index, own_w, t_of(t, k)).wait_recv()
        start(w_copy(1, k, index, w_slot(index), t_mate))

    def pass_c(ch):
        for k in range(1, half_l):
            index = l_of(l, -k)
            c_copy(0, k, ch, index, c_piece(c_ref, ch), l_of(l, k)).wait_recv()
            start(c_copy(1, k, ch, index, c_piece(cg.at[index], ch), l_mate))

    passed = 0
    for k in range(1, half_t):
        pass_w(k)
        while passed < chunks - 1 and passed * (half_t - 1) < k * (chunks - 1):
            pass_c(passed)
            passed += 1
    keep_w.wait()
    keep_c.wait()
    for k in range(half_t):
        w_copy(1, k, t_of(t_mate, -k), own_w, t_mate).wait_recv()

    rows = feat // 3
    for ch in range(chunks):
        if ch >= passed:
            pass_c(ch)
        for k in range(half_l):
            c_copy(1, k, ch, l_of(l_mate, -k), c_piece(c_ref, ch), l_mate).wait_recv()

        def body(m, carry, ch=ch):
            r0 = pl.multiple_of(m * rows, rows)
            total = None
            if joined:
                for b in range(n_lev):
                    part = jnp.dot(wg[b, pl.ds(r0, rows), :], cg[b, :, ch * width:(ch + 1) * width],
                                   preferred_element_type=jnp.float32)
                    total = part if total is None else total + part
            else:
                for b in range(n_tile):
                    k0 = (b % per) * cb
                    part = jnp.dot(wg[b, pl.ds(r0, rows), :],
                                   cg[b // per, k0:k0 + cb, ch * width:(ch + 1) * width],
                                   preferred_element_type=jnp.float32)
                    total = part if total is None else total + part
            g_ref[pl.ds(r0, rows), ch * width:(ch + 1) * width] = total.astype(jnp.bfloat16)
            return carry

        lax.fori_loop(0, 3, body, 0)
    for copy in sends:
        copy.wait_send()


def mix(c, w, n_tile, n_lev):
    feat, cells = c.shape
    cb = w.shape[1]
    chunks = 4
    w_shape = (n_lev, feat, feat) if cb % 128 == 0 else (n_tile, feat, cb)
    return pl.pallas_call(
        functools.partial(mix_kernel, n_tile, n_lev, chunks),
        out_shape=jax.ShapeDtypeStruct((feat, cells), jnp.bfloat16),
        in_specs=[pl.BlockSpec(memory_space=pl.ANY)] * 2,
        out_specs=pl.BlockSpec(memory_space=pltpu.VMEM),
        scratch_shapes=[
            pltpu.VMEM(w_shape, jnp.bfloat16),
            pltpu.VMEM((n_lev, feat, cells), jnp.bfloat16),
            pltpu.SemaphoreType.DMA((2,)),
            pltpu.SemaphoreType.DMA((2, n_tile // 2)),
            pltpu.SemaphoreType.DMA((2, n_tile // 2)),
            pltpu.SemaphoreType.DMA((2, n_lev // 2, chunks)),
            pltpu.SemaphoreType.DMA((2, n_lev // 2, chunks)),
        ],
        compiler_params=pltpu.CompilerParams(
            collective_id=0, has_side_effects=True, vmem_limit_bytes=48 * 2**20),
        name="mix",
    )(c, w)


def stencil_kernel(rows, cols, g_ref, k_ref, oh_ref, sel_ref, local_ref, vals_ref, top_ref, bottom_ref):
    g = g_ref[...]
    fb = g.shape[0]
    taps = k_ref[...]

    def tap(a, b):
        n = 3 * (a + 1) + b + 1
        return taps[:, n:n + 1]

    lane = lax.broadcasted_iota(jnp.int32, (fb, cols), 1)
    weight = {(a, b): jnp.broadcast_to(tap(a, b), (fb, cols)) for a in (-1, 0, 1) for b in (-1, 0, 1)}
    first, last = lane == 0, lane == cols - 1
    parts = {}
    top = bottom = None
    for r in range(rows + 1):
        if r < rows:
            mid = g[:, r * cols:(r + 1) * cols].astype(jnp.float32)
            after = jnp.where(last, 0.0, pltpu.roll(mid, cols - 1, 1))
            before = jnp.where(first, 0.0, pltpu.roll(mid, 1, 1))
            for a in (-1, 0, 1):
                parts[a, r] = weight[a, -1] * after + weight[a, 0] * mid + weight[a, 1] * before
        if r == 0:
            top = parts[-1, 0]
        else:
            i = r - 1
            total = parts[0, i]
            if i > 0:
                total = total + parts[1, i - 1]
            if i < rows - 1:
                total = total + parts[-1, i + 1]
            local_ref[:, i * cols:(i + 1) * cols] = total
    bottom = parts[1, rows - 1]
    top, bottom = top.astype(jnp.bfloat16), bottom.astype(jnp.bfloat16)
    top_ref[...] = top
    bottom_ref[...] = bottom
    edge = jnp.dot(g, sel_ref[...], preferred_element_type=jnp.float32)
    near = lane < cols // 2
    sides = jnp.where(near, weight[0, -1], weight[0, 1]) * edge
    sides += jnp.where(near, weight[-1, -1], weight[-1, 1]) * pltpu.roll(edge, cols - 1, 1)
    sides += jnp.where(near, weight[1, -1], weight[1, 1]) * pltpu.roll(edge, 1, 1)
    cycle = jnp.concatenate([top, bottom, sides.astype(jnp.bfloat16)], axis=1)
    vals_ref[...] = lax.dot_general(
        oh_ref[...], cycle, (((1,), (1,)), ((), ())), preferred_element_type=jnp.float32
    ).astype(jnp.bfloat16)


def deposit_kernel(rows, cols, local_ref, vals_ref, spread_ref, up_ref, down_ref, out_ref):
    total = local_ref[...] + lax.dot_general(
        vals_ref[...], spread_ref[...], (((0,), (0,)), ((), ())), preferred_element_type=jnp.float32)
    first = total[:, :cols] + up_ref[...].astype(jnp.float32)
    last = total[:, -cols:] + down_ref[...].astype(jnp.float32)
    total = jnp.concatenate([first, total[:, cols:-cols], last], axis=1)
    out_ref[...] = total.reshape(total.shape[0], rows, cols).astype(jnp.bfloat16)


def slot_place(slot, rows, cols):
    side, far = 2 * cols, 2 * cols + cols // 2
    low = slot - (cols + 2)
    place = jnp.where(slot < cols + 2, slot - 1, cols + low - 1)
    place = jnp.where(slot == 0, side, place)
    place = jnp.where(slot == cols + 1, far, place)
    place = jnp.where(low == 0, side + rows + 1, place)
    place = jnp.where(low == cols + 1, far + rows + 1, place)
    left = slot - 2 * (cols + 2)
    place = jnp.where(left >= 0, side + 1 + left, place)
    place = jnp.where(left >= rows, far + 1 + left - rows, place)
    return jnp.where(slot < 0, -1, place)


def per_device(cotangent, mix_weight, kernel, send_rows, recv_cells, recv_weight, n_tile, n_lev):
    feat, rows, cols = cotangent.shape
    cells = rows * cols
    most = send_rows.shape[2]
    pad = -(-most // 16) * 16
    strips = n_tile // 2
    tile_here = lax.axis_index("tile")
    place = (tile_here + strips // 2) % n_tile % strips
    extra = ((0, 0), (0, pad - most))
    places = jnp.pad(slot_place(send_rows[0], rows, cols), extra, constant_values=-1).reshape(-1, 1)
    picks = (places == jnp.arange(3 * cols, dtype=jnp.int32)[None, :]).astype(jnp.bfloat16)
    targets = jnp.pad(recv_cells[0], extra, constant_values=-1).reshape(-1, 1)
    weights = jnp.pad(recv_weight[0], ((0, 0),) + extra).reshape(4, -1, 1)
    at = jnp.arange(cells, dtype=jnp.int32)[None, :] - targets
    spread = jnp.zeros(at.shape, jnp.float32)
    for corner, offset in enumerate((0, 1, cols, cols + 1)):
        spread = jnp.where((at == offset) & (targets >= 0), weights[corner], spread)
    spread = spread.astype(jnp.bfloat16)
    cell = jnp.arange(cells, dtype=jnp.int32)[:, None]
    spot = jnp.arange(cols, dtype=jnp.int32)[None, :]
    row, col = cell // cols, cell % cols
    select = ((col == 0) & (spot == row + 1)) | ((col == cols - 1) & (spot == cols // 2 + row + 1))
    select = select.astype(jnp.bfloat16)

    grad = mix(cotangent.reshape(feat, cells), mix_weight, n_tile, n_lev)

    fb = 128
    entries = picks.shape[0]
    grid = (feat // fb,)
    by_feat = lambda width: pl.BlockSpec((fb, width), lambda i: (i, 0))
    whole = lambda shape: pl.BlockSpec(shape, lambda i: (0, 0))
    by_column = pl.BlockSpec((entries, fb), lambda i: (0, i))
    params = pltpu.CompilerParams(vmem_limit_bytes=48 * 2**20)
    local, vals, top, bottom = pl.pallas_call(
        functools.partial(stencil_kernel, rows, cols),
        grid=grid,
        out_shape=[
            jax.ShapeDtypeStruct((feat, cells), jnp.float32),
            jax.ShapeDtypeStruct((entries, feat), jnp.bfloat16),
            jax.ShapeDtypeStruct((feat, cols), jnp.bfloat16),
            jax.ShapeDtypeStruct((feat, cols), jnp.bfloat16),
        ],
        in_specs=[by_feat(cells), by_feat(9), whole((entries, 3 * cols)), whole((cells, cols))],
        out_specs=[by_feat(cells), by_column, by_feat(cols), by_feat(cols)],
        compiler_params=params,
        name="stencil",
    )(grad, kernel, picks, select)
    up = lax.ppermute(bottom, "tile", [(i, (i + 1) % n_tile) for i in range(n_tile)])
    down = lax.ppermute(top, "tile", [((i + 1) % n_tile, i) for i in range(n_tile)])
    up = jnp.where(place != 0, up, jnp.zeros_like(up))
    down = jnp.where(place != strips - 1, down, jnp.zeros_like(down))
    vals = lax.all_to_all(vals, "tile", split_axis=0, concat_axis=0, tiled=True)
    return pl.pallas_call(
        functools.partial(deposit_kernel, rows, cols),
        grid=grid,
        out_shape=jax.ShapeDtypeStruct((feat, rows, cols), jnp.bfloat16),
        in_specs=[by_feat(cells), by_column, whole((entries, cells)), by_feat(cols), by_feat(cols)],
        out_specs=pl.BlockSpec((fb, rows, cols), lambda i: (i, 0, 0)),
        compiler_params=params,
        name="deposit",
    )(local, vals, spread, up, down)


def solution(mesh):
    in_specs = (
        P("lev", "tile", None),
        P(None, "tile"),
        P("lev", None),
        P("tile", None, None),
        P("tile", None, None),
        P("tile", None, None, None),
    )
    return jax.shard_map(
        functools.partial(per_device, n_tile=mesh.shape["tile"], n_lev=mesh.shape["lev"]),
        mesh=mesh, in_specs=in_specs, out_specs=P("lev", "tile", None), check_vma=False)
```

time: 364 us -> 144 us (0.40)
  the two profiles are of different devices: /device:TPU:17 before, /device:TPU:0 now
where the time goes in v1:
time: 144 us
  Pallas kernels  98.2 us (68%)
  starting transfers between devices  20.9 us (15%)
  waiting for transfers between devices  13.3 us (9%)
  local copies, waits for them, and re-layouts  5.74 us (4%)
  other arithmetic  5.36 us (4%)
    pallas_call x1, Pallas kernels, mix(): pl.pallas_call(functools.partial(mix_kernel, n_tile, n_lev, chunks), out_...  82.9 us
    ppermute x1, starting transfers between devices, per_device(): lax.ppermute(top, 'tile', [((i + 1) % n_tile, i) for i in range(n_tile)])  14.9 us
    all_to_all x1, waiting for transfers between devices, per_device(): vals = lax.all_to_all(vals, 'tile', split_axis=0, concat_axis=0, tiled=True)  13.3 us
    pallas_call x1, Pallas kernels, per_device(): pl.pallas_call(functools.partial(stencil_kernel, rows, cols), grid=grid,...  7.95 us
    pallas_call x1, Pallas kernels, per_device(): pl.pallas_call(functools.partial(deposit_kernel, rows, cols), grid=grid,...  7.34 us
    all_to_all x1, starting transfers between devices, per_device(): vals = lax.all_to_all(vals, 'tile', split_axis=0, concat_axis=0, tiled=True)  6 us
    unnamed x12, local copies, waits for them, and re-layouts  5.22 us
    convert_element_type x1, other arithmetic, per_device(): spread = spread.astype(jnp.bfloat16)  3.3 us
  transfers between devices with their start and end apart: 3, of which 1 were waited for; matrix products, arithmetic and copies ran while one was open for 3% of the time, Pallas kernels for 0%

profile of v1, /device:TPU:0, one launch (start us, length us, event | category | flops | bytes accessed | tf_op | source)
XLA Modules:
  0.0 143.8 jit_solution(14599972812530534350)
XLA Ops:
  0.0 0.0 copy-start.1
  0.0 0.0 copy-start.3
  0.0 0.0 copy-start
  0.0 5.0 %copy.10 = bf16[96,8,16,128]{3,1,2,0:T(8,128)(2,1)} copy(bf16[96,8,16,128]{3,2,1,0:T(8,128)(2,1)} %bitcast.46) | data formatting | bytes 6291456
  5.1 0.0 copy-done.1
  5.1 0.2 copy.7.k_ref
  5.2 0.0 copy-done.3
  5.3 0.1 eq.118
  5.4 0.1 fusion.12.oh_ref
  5.5 0.0 copy-done
  5.5 82.9 %mix.1.g_ref = bf16[768,2048]{1,0:T(8,128)(2,1)S(1)} custom-call(bf16[768,2048]{1,0:T(8,128)(2,1)} %bitcast.45, bf16[3072,384]{1,0:T(8,128)(2,1)S(1)} %copy-done), custom_call_target="tpu_custom_call" | custom-call | tf_op jit(solution)/shard_map/mix/pallas_call | solution.py:134
  88.5 0.0 copy-start.4
  88.5 0.0 copy-start.2
  88.5 1.9 %fusion.10.sel_ref = bf16[2048,128]{1,0:T(8,128)(2,1)S(1)} fusion(s32[2048]{0:T(1024)S(1)} %get-tuple-element.17, s32[2048]{0:T(1024)S(1)} %get-tuple-element.18, pred[2048]{0:T(1024)(128)(4,1)S(1)} %get-tuple-element.19, pred[2048]{0:T(1024)(128)(4,1)S(1)} %get-tuple-element.20), kind=kLoop, calls=%fused_computation.15 | loop fusion | flops 1572864 | bytes 544768 | tf_op jit(solution)/shard_map/convert_element_type | solution.py:245
  90.4 7.9 %stencil.1 = (f32[768,2048]{1,0:T(8,128)}, bf16[384,768]{1,0:T(8,128)(2,1)}, bf16[768,128]{1,0:T(8,128)(2,1)S(1)}, bf16[768,128]{1,0:T(8,128)(2,1)S(1)}) custom-call(bf16[768,2048]{1,0:T(8,128)(2,1)S(1)} %mix.1.g_ref, f32[768,9]{1,0:T(8,128)S(1)} %copy.7.k_ref, bf16[384,384]{1,0:T(8,128)(2,1)S(1)} %fusion.12.oh_ref, bf16[2048,128]{1,0:T(8,128)(2,1)S(1)} %fusion.10.sel_ref), custom_call_target="tpu_custom_call" | custom-call | tf_op jit(solution)/shard_map/stencil/pallas_call | solution.py:256
  98.3 14.9 %collective-permute-start.1 = (bf16[768,128]{1,0:T(8,128)(2,1)S(1)}, bf16[768,128]{1,0:T(8,128)(2,1)S(1)}, u32[]{:S(2)}, u32[]{:S(2)}) collective-permute-start(bf16[768,128]{1,0:T(8,128)(2,1)S(1)} %get-tuple-element.12), channel_id=1, source_target_pairs={{4,0},{8,4},{12,8},{16,12},{20,16},{24,20},{28,24},{0,28},{5,1},{9... | collective-permute-start | bytes 589832 | tf_op jit(solution)/shard_map/ppermute | solution.py:271
  113.2 0.0 collective-permute-start
  113.2 6.0 %all-to-all-start = ((bf16[8,48,768]{2,1,0:T(8,128)(2,1)}), bf16[8,48,768]{2,1,0:T(8,128)(2,1)S(1)}, u32[]{:S(2)}, u32[]{:S(2)}) async-start(bf16[8,48,768]{2,1,0:T(8,128)(2,1)} %bitcast.11), calls=%async_computation | async-start | bytes 1179648 | tf_op jit(solution)/shard_map/all_to_all | solution.py:274
  119.2 0.0 copy-done.4
  119.2 0.1 sub.50
  119.3 0.0 copy-done.2
  119.3 0.1 broadcast_in_dim.62
  119.4 0.1 broadcast_in_dim.64
  119.5 0.1 broadcast_in_dim.66
  119.6 0.1 broadcast_in_dim.68
  119.7 3.3 %select_convert_fusion.spread_ref = bf16[384,2048]{1,0:T(8,128)(2,1)S(1)} fusion(bf16[384]{0:T(512)(128)(2,1)S(1)} %broadcast_in_dim.68, bf16[384]{0:T(512)(128)(2,1)S(1)} %broadcast_in_dim.66, bf16[384]{0:T(512)(128)(2,1)S(1)} %broadcast_in_dim.64, bf16[384]{0:T(512)(128)(2,1)S(1)} %broadcast_in_dim.62, s32[384]{0:T(512)S(1)} %sub.50, ...), kind=kLoop, calls=%fused_computation.1 | loop fusion | flops 10223616 | bytes 1577856 | tf_op jit(solution)/shard_map/convert_element_type | solution.py:240
  123.0 0.0 collective-permute-done.1
  123.0 0.0 collective-permute-done
  123.1 13.3 %all-to-all-done = bf16[8,48,768]{2,1,0:T(8,128)(2,1)S(1)} async-done(((bf16[8,48,768]{2,1,0:T(8,128)(2,1)}), bf16[8,48,768]{2,1,0:T(8,128)(2,1)S(1)}, u32[]{:S(2)}, u32[]{:S(2)}) %all-to-all-start) | async-done | bytes 589856 | tf_op jit(solution)/shard_map/all_to_all | solution.py:274
  136.4 7.3 %deposit.1 = bf16[768,16,128]{2,1,0:T(8,128)(2,1)} custom-call(f32[768,2048]{1,0:T(8,128)} %get-tuple-element.9.local_ref, bf16[384,768]{1,0:T(8,128)(2,1)S(1)} %bitcast.44, bf16[384,2048]{1,0:T(8,128)(2,1)S(1)} %select_convert_fusion.spread_ref, bf16[768,128]{1,0:T(8,128)(2,1)S(1)} %broadcast_select_fusion.1.up_ref, ...), custom_call_target="tpu_custom_call" | custom-call | tf_op jit(solution)/shard_map/deposit/pallas_call | solution.py:275
  (9 shorter events, 0.1 us)
Async XLA Ops:
  0.0 5.0 %copy-start.1 = (f32[768,9]{0,1:T(8,128)S(1)}, f32[768,9]{0,1:T(8,128)}, u32[]{:S(2)}) copy-start(f32[768,9]{0,1:T(8,128)} %param.8) | copy-start | bytes 82948
  0.0 5.2 %copy-start.3 = (s32[1,8,41]{2,1,0:T(8,128)S(1)}, s32[1,8,41]{2,1,0:T(8,128)}, u32[]{:S(2)}) copy-start(s32[1,8,41]{2,1,0:T(8,128)} %param.9) | copy-start | bytes 3940
  0.0 5.5 %copy-start = (bf16[3072,384]{1,0:T(8,128)(2,1)S(1)}, bf16[3072,384]{1,0:T(8,128)(2,1)}, u32[]{:S(2)}) copy-start(bf16[3072,384]{1,0:T(8,128)(2,1)} %w_ref.1) | copy-start | bytes 7077892
  88.5 30.7 %copy-start.4 = (s32[1,8,41]{2,1,0:T(8,128)S(1)}, s32[1,8,41]{2,1,0:T(8,128)}, u32[]{:S(2)}) copy-start(s32[1,8,41]{2,1,0:T(8,128)} %param.10) | copy-start | bytes 3940
  88.5 30.8 %copy-start.2 = (f32[1,4,8,41]{3,2,1,0:T(8,128)S(1)}, f32[1,4,8,41]{3,2,1,0:T(8,128)}, u32[]{:S(2)}) copy-start(f32[1,4,8,41]{3,2,1,0:T(8,128)} %param.11) | copy-start | bytes 15748
  98.3 24.7 %collective-permute-start.1 = (bf16[768,128]{1,0:T(8,128)(2,1)S(1)}, bf16[768,128]{1,0:T(8,128)(2,1)S(1)}, u32[]{:S(2)}, u32[]{:S(2)}) collective-permute-start(bf16[768,128]{1,0:T(8,128)(2,1)S(1)} %get-tuple-element.12), channel_id=1, source_target_pairs={{4,0},{8,4},{12,8},{16,12},{20,16},{24,20},{28,24},{0,28},{5,1},{9... | collective-permute-start | bytes 589832 | tf_op jit(solution)/shard_map/ppermute | solution.py:271
  113.2 9.9 %collective-permute-start = (bf16[768,128]{1,0:T(8,128)(2,1)S(1)}, bf16[768,128]{1,0:T(8,128)(2,1)S(1)}, u32[]{:S(2)}, u32[]{:S(2)}) collective-permute-start(bf16[768,128]{1,0:T(8,128)(2,1)S(1)} %get-tuple-element.11), channel_id=1, source_target_pairs={{0,4},{4,8},{8,12},{12,16},{16,20},{20,24},{24,28},{28,0},{1,5},{5... | collective-permute-start | bytes 589832 | tf_op jit(solution)/shard_map/ppermute | solution.py:270
  113.2 23.2 %all-to-all-start = ((bf16[8,48,768]{2,1,0:T(8,128)(2,1)}), bf16[8,48,768]{2,1,0:T(8,128)(2,1)S(1)}, u32[]{:S(2)}, u32[]{:S(2)}) async-start(bf16[8,48,768]{2,1,0:T(8,128)(2,1)} %bitcast.11), calls=%async_computation | async-start | bytes 1179648 | tf_op jit(solution)/shard_map/all_to_all | solution.py:274

commit v2 on v1

--- a/solution.py
+++ b/solution.py
@@ -10,7 +10,10 @@
 MESH = pl.DeviceIdType.MESH
 
 
-def mix_kernel(n_tile, n_lev, chunks, c_ref, w_ref, g_ref, wg, cg, local_sem, ws, wr, cs, cr):
+def mix_kernel(n_tile, n_lev, chunks, rows_n, cols, c_ref, w_ref, k_ref, oh_ref, cell_ref, weight_ref,
+               local_out, vals_out, up_out, down_out, spread_out,
+               g_ref, local_ref, vals_ref, top_ref, bottom_ref, spread_ref, sel_ref,
+               wg, cg, local_sem, ws, wr, cs, cr, es, er):
     t = lax.axis_index("tile")
     l = lax.axis_index("lev")
     feat, cells = c_ref.shape
@@ -29,7 +32,7 @@
         return lax.rem(base + 2 * k + 2 * n_lev, n_lev)
 
     barrier = pltpu.get_barrier_semaphore()
-    peers = [(t_of(t, k), l) for k in range(1, half_t)] + [(t_mate, l), (t, l_mate)]
+    peers = [(lax.rem(t + k, n_tile), l) for k in range(1, n_tile)] + [(t, l_mate)]
     peers += [(t, l_of(l, k)) for k in range(1, half_l)]
     for peer in peers:
         pl.semaphore_signal(barrier, inc=1, device_id=peer, device_id_type=MESH)
@@ -73,6 +76,28 @@
     keep_c = pltpu.make_async_copy(c_ref, cg.at[l], local_sem.at[1])
     keep_w.start()
     keep_c.start()
+
+    entries = cell_ref.shape[0]
+
+    def fill(b, carry):
+        r0 = pl.multiple_of(b * 16, 16)
+        cell = cell_ref[pl.ds(r0, 16), :]
+        at = lax.broadcasted_iota(jnp.int32, (16, cells), 1) - cell
+        weights = weight_ref[pl.ds(r0, 16), :]
+        total = jnp.zeros((16, cells), jnp.float32)
+        for corner, offset in enumerate((0, 1, cols, cols + 1)):
+            total = jnp.where(at == offset, weights[:, corner:corner + 1], total)
+        spread_ref[pl.ds(r0, 16), :] = jnp.where(cell >= 0, total, 0.0).astype(jnp.bfloat16)
+        return carry
+
+    lax.fori_loop(0, entries // 16, fill, 0)
+    keep_spread = pltpu.make_async_copy(spread_ref, spread_out, local_sem.at[2])
+    keep_spread.start()
+    col = lax.broadcasted_iota(jnp.int32, (cols, cols), 0)
+    spot = lax.broadcasted_iota(jnp.int32, (cols, cols), 1)
+    for r in range(rows_n):
+        hit = ((col == 0) & (spot == r + 1)) | ((col == cols - 1) & (spot == cols // 2 + r + 1))
+        sel_ref[r * cols:(r + 1) * cols, :] = jnp.where(hit, 1.0, 0.0).astype(jnp.bfloat16)
 
     def pass_w(k):
         index = t_of(t, -k)
@@ -122,39 +147,101 @@
             return carry
 
         lax.fori_loop(0, 3, body, 0)
+
+    strips = n_tile // 2
+    q = lax.rem(t + strips // 2, n_tile)
+    panel, place = q // strips, lax.rem(q, strips)
+    keep_top = (place != 0).astype(jnp.float32)
+    keep_bottom = (place != strips - 1).astype(jnp.float32)
+
+    def shape(m, carry):
+        stencil(rows_n, cols, pl.ds(pl.multiple_of(m * 128, 128), 128), keep_top, keep_bottom,
+                g_ref, k_ref, oh_ref, sel_ref, local_ref, vals_ref, top_ref, bottom_ref)
+        return carry
+
+    lax.fori_loop(0, feat // 128, shape, 0)
+    pad = entries // strips
+    edge_copies = [
+        pltpu.make_async_remote_copy(
+            src_ref=top_ref, dst_ref=down_out, send_sem=es.at[0], recv_sem=er.at[0],
+            device_id=(lax.rem(t + n_tile - 1, n_tile), l), device_id_type=MESH),
+        pltpu.make_async_remote_copy(
+            src_ref=bottom_ref, dst_ref=up_out, send_sem=es.at[1], recv_sem=er.at[1],
+            device_id=(lax.rem(t + 1, n_tile), l), device_id_type=MESH),
+    ]
+
+    def vals_copy(j, slot):
+        to = lax.rem((1 - panel) * strips + j - strips // 2 + n_tile, n_tile)
+        return pltpu.make_async_remote_copy(
+            src_ref=vals_ref.at[pl.ds(j * pad, pad)],
+            dst_ref=vals_out.at[pl.ds(pl.multiple_of(slot * pad, 16), pad)],
+            send_sem=es.at[2 + j], recv_sem=er.at[2 + slot], device_id=(to, l), device_id_type=MESH)
+
+    for copy in edge_copies:
+        start(copy)
+    for j in range(strips):
+        start(vals_copy(j, place))
+    keep_local = pltpu.make_async_copy(local_ref, local_out, local_sem.at[3])
+    keep_local.start()
+    for copy in edge_copies:
+        copy.wait_recv()
+    for j in range(strips):
+        vals_copy(j, j).wait_recv()
+    keep_spread.wait()
+    keep_local.wait()
     for copy in sends:
         copy.wait_send()
 
 
-def mix(c, w, n_tile, n_lev):
+def mix(c, w, kernel, picks, targets, weights, n_tile, n_lev, rows, cols):
     feat, cells = c.shape
     cb = w.shape[1]
     chunks = 4
+    entries = picks.shape[0]
+    strips = n_tile // 2
     w_shape = (n_lev, feat, feat) if cb % 128 == 0 else (n_tile, feat, cb)
+    vmem = pl.BlockSpec(memory_space=pltpu.VMEM)
+    anywhere = pl.BlockSpec(memory_space=pl.ANY)
     return pl.pallas_call(
-        functools.partial(mix_kernel, n_tile, n_lev, chunks),
-        out_shape=jax.ShapeDtypeStruct((feat, cells), jnp.bfloat16),
-        in_specs=[pl.BlockSpec(memory_space=pl.ANY)] * 2,
-        out_specs=pl.BlockSpec(memory_space=pltpu.VMEM),
+        functools.partial(mix_kernel, n_tile, n_lev, chunks, rows, cols),
+        out_shape=[
+            jax.ShapeDtypeStruct((feat, cells), jnp.float32),
+            jax.ShapeDtypeStruct((entries, feat), jnp.bfloat16),
+            jax.ShapeDtypeStruct((feat, cols), jnp.bfloat16),
+            jax.ShapeDtypeStruct((feat, cols), jnp.bfloat16),
+            jax.ShapeDtypeStruct((entries, cells), jnp.bfloat16),
+        ],
+        in_specs=[anywhere] * 2 + [vmem] * 4,
+        out_specs=[anywhere] * 5,
         scratch_shapes=[
+            pltpu.VMEM((feat, cells), jnp.bfloat16),
+            pltpu.VMEM((feat, cells), jnp.float32),
+            pltpu.VMEM((entries, feat), jnp.bfloat16),
+            pltpu.VMEM((feat, cols), jnp.bfloat16),
+            pltpu.VMEM((feat, cols), jnp.bfloat16),
+            pltpu.VMEM((entries, cells), jnp.bfloat16),
+            pltpu.VMEM((cells, cols), jnp.bfloat16),
             pltpu.VMEM(w_shape, jnp.bfloat16),
             pltpu.VMEM((n_lev, feat, cells), jnp.bfloat16),
-            pltpu.SemaphoreType.DMA((2,)),
+            pltpu.SemaphoreType.DMA((4,)),
             pltpu.SemaphoreType.DMA((2, n_tile // 2)),
             pltpu.SemaphoreType.DMA((2, n_tile // 2)),
             pltpu.SemaphoreType.DMA((2, n_lev // 2, chunks)),
             pltpu.SemaphoreType.DMA((2, n_lev // 2, chunks)),
+            pltpu.SemaphoreType.DMA((2 + strips,)),
+            pltpu.SemaphoreType.DMA((2 + strips,)),
         ],
         compiler_params=pltpu.CompilerParams(
-            collective_id=0, has_side_effects=True, vmem_limit_bytes=48 * 2**20),
+            collective_id=0, has_side_effects=True, vmem_limit_bytes=52 * 2**20),
         name="mix",
-    )(c, w)
-
-
-def stencil_kernel(rows, cols, g_ref, k_ref, oh_ref, sel_ref, local_ref, vals_ref, top_ref, bottom_ref):
-    g = g_ref[...]
+    )(c, w, kernel, picks, targets, weights)
+
+
+def stencil(rows, cols, part, keep_top, keep_bottom,
+            g_ref, k_ref, oh_ref, sel_ref, local_ref, vals_ref, top_ref, bottom_ref):
+    g = g_ref[part, :]
     fb = g.shape[0]
-    taps = k_ref[...]
+    taps = k_ref[part, :]
 
     def tap(a, b):
         n = 3 * (a + 1) + b + 1
@@ -181,18 +268,18 @@
                 total = total + parts[1, i - 1]
             if i < rows - 1:
                 total = total + parts[-1, i + 1]
-            local_ref[:, i * cols:(i + 1) * cols] = total
+            local_ref[part, i * cols:(i + 1) * cols] = total
     bottom = parts[1, rows - 1]
+    top_ref[part, :] = (top * keep_top).astype(jnp.bfloat16)
+    bottom_ref[part, :] = (bottom * keep_bottom).astype(jnp.bfloat16)
     top, bottom = top.astype(jnp.bfloat16), bottom.astype(jnp.bfloat16)
-    top_ref[...] = top
-    bottom_ref[...] = bottom
     edge = jnp.dot(g, sel_ref[...], preferred_element_type=jnp.float32)
     near = lane < cols // 2
     sides = jnp.where(near, weight[0, -1], weight[0, 1]) * edge
     sides += jnp.where(near, weight[-1, -1], weight[-1, 1]) * pltpu.roll(edge, cols - 1, 1)
     sides += jnp.where(near, weight[1, -1], weight[1, 1]) * pltpu.roll(edge, 1, 1)
     cycle = jnp.concatenate([top, bottom, sides.astype(jnp.bfloat16)], axis=1)
-    vals_ref[...] = lax.dot_general(
+    vals_ref[:, part] = lax.dot_general(
         oh_ref[...], cycle, (((1,), (1,)), ((), ())), preferred_element_type=jnp.float32
     ).astype(jnp.bfloat16)
 
@@ -226,25 +313,21 @@
     most = send_rows.shape[2]
     pad = -(-most // 16) * 16
     strips = n_tile // 2
-    tile_here = lax.axis_index("tile")
-    place = (tile_here + strips // 2) % n_tile % strips
-    extra = ((0, 0), (0, pad - most))
-    places = jnp.pad(slot_place(send_rows[0], rows, cols), extra, constant_values=-1).reshape(-1, 1)
+    panel = (lax.axis_index("tile") + strips // 2) % n_tile // strips
+    begin = ((1 - panel) * strips - strips // 2 + n_tile) % n_tile
+
+    def of_partners(table, dim):
+        table = lax.dynamic_slice_in_dim(jnp.concatenate([table, table], axis=dim), begin, strips, dim)
+        width = [(0, 0)] * (table.ndim - 1) + [(0, pad - most)]
+        return jnp.pad(table, width, constant_values=-1)
+
+    places = slot_place(of_partners(send_rows[0], 0), rows, cols).reshape(-1, 1)
     picks = (places == jnp.arange(3 * cols, dtype=jnp.int32)[None, :]).astype(jnp.bfloat16)
-    targets = jnp.pad(recv_cells[0], extra, constant_values=-1).reshape(-1, 1)
-    weights = jnp.pad(recv_weight[0], ((0, 0),) + extra).reshape(4, -1, 1)
-    at = jnp.arange(cells, dtype=jnp.int32)[None, :] - targets
-    spread = jnp.zeros(at.shape, jnp.float32)
-    for corner, offset in enumerate((0, 1, cols, cols + 1)):
-        spread = jnp.where((at == offset) & (targets >= 0), weights[corner], spread)
-    spread = spread.astype(jnp.bfloat16)
-    cell = jnp.arange(cells, dtype=jnp.int32)[:, None]
-    spot = jnp.arange(cols, dtype=jnp.int32)[None, :]
-    row, col = cell // cols, cell % cols
-    select = ((col == 0) & (spot == row + 1)) | ((col == cols - 1) & (spot == cols // 2 + row + 1))
-    select = select.astype(jnp.bfloat16)
-
-    grad = mix(cotangent.reshape(feat, cells), mix_weight, n_tile, n_lev)
+    targets = of_partners(recv_cells[0], 0).reshape(-1, 1)
+    weights = of_partners(recv_weight[0], 1).reshape(4, -1).T
+
+    local, vals, up, down, spread = mix(
+        cotangent.reshape(feat, cells), mix_weight, kernel, picks, targets, weights, n_tile, n_lev, rows, cols)
 
     fb = 128
     entries = picks.shape[0]
@@ -253,25 +336,6 @@
     whole = lambda shape: pl.BlockSpec(shape, lambda i: (0, 0))
     by_column = pl.BlockSpec((entries, fb), lambda i: (0, i))
     params = pltpu.CompilerParams(vmem_limit_bytes=48 * 2**20)
-    local, vals, top, bottom = pl.pallas_call(
-        functools.partial(stencil_kernel, rows, cols),
-        grid=grid,
-        out_shape=[
-            jax.ShapeDtypeStruct((feat, cells), jnp.float32),
-            jax.ShapeDtypeStruct((entries, feat), jnp.bfloat16),
-            jax.ShapeDtypeStruct((feat, cols), jnp.bfloat16),
-            jax.ShapeDtypeStruct((feat, cols), jnp.bfloat16),
-        ],
-        in_specs=[by_feat(cells), by_feat(9), whole((entries, 3 * cols)), whole((cells, cols))],
-        out_specs=[by_feat(cells), by_column, by_feat(cols), by_feat(cols)],
-        compiler_params=params,
-        name="stencil",
-    )(grad, kernel, picks, select)
-    up = lax.ppermute(bottom, "tile", [(i, (i + 1) % n_tile) for i in range(n_tile)])
-    down = lax.ppermute(top, "tile", [((i + 1) % n_tile, i) for i in range(n_tile)])
-    up = jnp.where(place != 0, up, jnp.zeros_like(up))
-    down = jnp.where(place != strips - 1, down, jnp.zeros_like(down))
-    vals = lax.all_to_all(vals, "tile", split_axis=0, concat_axis=0, tiled=True)
     return pl.pallas_call(
         functools.partial(deposit_kernel, rows, cols),
         grid=grid,

time: 144 us -> 130 us (0.903)
  the two profiles are of different devices: /device:TPU:0 before, /device:TPU:17 now
where the time goes in v2:
time: 130 us
  Pallas kernels  121 us (93%)
  local copies, waits for them, and re-layouts  7.31 us (6%)
  other arithmetic  1.68 us (1%)
    pallas_call x1, Pallas kernels, mix(): pl.pallas_call(functools.partial(mix_kernel, n_tile, n_lev, chunks, rows,...  114 us
    unnamed x5, local copies, waits for them, and re-layouts  7.09 us
    pallas_call x1, Pallas kernels, per_device(): pl.pallas_call(functools.partial(deposit_kernel, rows, cols), grid=grid,...  6.99 us

profile of v2, /device:TPU:17, one launch (start us, length us, event | category | flops | bytes accessed | tf_op | source)
XLA Modules:
  0.0 129.7 jit_solution(14609885675251408032)
XLA Ops:
  0.0 0.8 fusion.2
  0.8 0.1 eq.34
  0.9 0.8 fusion.1
  1.7 0.1 copy.12
  1.8 0.1 reshape.14.cell_ref
  2.0 0.1 fusion.oh_ref
  2.1 1.0 copy.10.k_ref
  3.0 4.9 %copy.15 = bf16[96,8,16,128]{3,1,2,0:T(8,128)(2,1)} copy(bf16[96,8,16,128]{3,2,1,0:T(8,128)(2,1)} %bitcast.12) | data formatting | bytes 6291456
  7.9 113.7 %mix.1 = (f32[768,2048]{1,0:T(8,128)}, bf16[192,768]{1,0:T(8,128)(2,1)S(1)}, bf16[768,128]{1,0:T(8,128)(2,1)S(1)}, bf16[768,128]{1,0:T(8,128)(2,1)S(1)}, bf16[192,2048]{1,0:T(8,128)(2,1)}) custom-call(bf16[768,2048]{1,0:T(8,128)(2,1)} %bitcast.11, bf16[3072,384]{1,0:T(8,128)(2,1)} %w_ref.1, f32[768,9]{1,0:T(8,128)S(1)} %copy.10.k_ref, ...), custom_call_target="tpu_custom_call" | custom-call | tf_op jit(solution)/shard_map/mix/pallas_call | solution.py:205
  121.6 0.0 copy-start
  121.6 1.1 copy-done
  122.8 7.0 %deposit.1 = bf16[768,16,128]{2,1,0:T(8,128)(2,1)} custom-call(f32[768,2048]{1,0:T(8,128)} %get-tuple-element.10.local_ref, bf16[192,768]{1,0:T(8,128)(2,1)S(1)} %get-tuple-element.11.vals_ref, bf16[192,2048]{1,0:T(8,128)(2,1)S(1)} %copy-done, bf16[768,128]{1,0:T(8,128)(2,1)S(1)} %get-tuple-element.13.up_ref, bf16[768,128]{1,0:T(8,128)(2,1)S(1)} %get-tuple-element.14.down_ref), custom_call_target="tpu_custom_call" | custom-call | tf_op jit(solution)/shard_map/deposit/pallas_call | solution.py:339
  (3 shorter events, 0.0 us)
Async XLA Ops:
  121.6 1.1 copy-start

commit v3 on v2

--- a/solution.py
+++ b/solution.py
@@ -122,6 +122,25 @@
         w_copy(1, k, t_of(t_mate, -k), own_w, t_mate).wait_recv()
 
     rows = feat // 3
+    span = width // cols
+    kept = []
+
+    def run_interior(ch):
+        low = max(ch * span - 1, 0)
+        high = rows_n if ch == chunks - 1 else (ch + 1) * span - 1
+
+        def step(m, carry):
+            part = pl.ds(pl.multiple_of(m * 128, 128), 128)
+            interior(rows_n, cols, low, high, part, g_ref, k_ref, local_ref)
+            return carry
+
+        lax.fori_loop(0, feat // 128, step, 0)
+        copy = pltpu.make_async_copy(
+            local_ref.at[:, low * cols:high * cols], local_out.at[:, low * cols:high * cols],
+            local_sem.at[3 + ch])
+        copy.start()
+        kept.append(copy)
+
     for ch in range(chunks):
         if ch >= passed:
             pass_c(ch)
@@ -147,6 +166,8 @@
             return carry
 
         lax.fori_loop(0, 3, body, 0)
+        if ch < chunks - 1:
+            run_interior(ch)
 
     strips = n_tile // 2
     q = lax.rem(t + strips // 2, n_tile)
@@ -155,8 +176,8 @@
     keep_bottom = (place != strips - 1).astype(jnp.float32)
 
     def shape(m, carry):
-        stencil(rows_n, cols, pl.ds(pl.multiple_of(m * 128, 128), 128), keep_top, keep_bottom,
-                g_ref, k_ref, oh_ref, sel_ref, local_ref, vals_ref, top_ref, bottom_ref)
+        edges(rows_n, cols, pl.ds(pl.multiple_of(m * 128, 128), 128), keep_top, keep_bottom,
+              g_ref, k_ref, oh_ref, sel_ref, vals_ref, top_ref, bottom_ref)
         return carry
 
     lax.fori_loop(0, feat // 128, shape, 0)
@@ -181,14 +202,14 @@
         start(copy)
     for j in range(strips):
         start(vals_copy(j, place))
-    keep_local = pltpu.make_async_copy(local_ref, local_out, local_sem.at[3])
-    keep_local.start()
+    run_interior(chunks - 1)
     for copy in edge_copies:
         copy.wait_recv()
     for j in range(strips):
         vals_copy(j, j).wait_recv()
     keep_spread.wait()
-    keep_local.wait()
+    for copy in kept:
+        copy.wait()
     for copy in sends:
         copy.wait_send()
 
@@ -223,7 +244,7 @@
             pltpu.VMEM((cells, cols), jnp.bfloat16),
             pltpu.VMEM(w_shape, jnp.bfloat16),
             pltpu.VMEM((n_lev, feat, cells), jnp.bfloat16),
-            pltpu.SemaphoreType.DMA((4,)),
+            pltpu.SemaphoreType.DMA((3 + chunks,)),
             pltpu.SemaphoreType.DMA((2, n_tile // 2)),
             pltpu.SemaphoreType.DMA((2, n_tile // 2)),
             pltpu.SemaphoreType.DMA((2, n_lev // 2, chunks)),
@@ -237,48 +258,56 @@
     )(c, w, kernel, picks, targets, weights)
 
 
-def stencil(rows, cols, part, keep_top, keep_bottom,
-            g_ref, k_ref, oh_ref, sel_ref, local_ref, vals_ref, top_ref, bottom_ref):
-    g = g_ref[part, :]
-    fb = g.shape[0]
+def shifted(g_ref, part, r, cols):
+    mid = g_ref[part, r * cols:(r + 1) * cols].astype(jnp.float32)
+    lane = lax.broadcasted_iota(jnp.int32, mid.shape, 1)
+    after = jnp.where(lane == cols - 1, 0.0, pltpu.roll(mid, cols - 1, 1))
+    before = jnp.where(lane == 0, 0.0, pltpu.roll(mid, 1, 1))
+    return after, mid, before
+
+
+def taps_of(k_ref, part, cols):
     taps = k_ref[part, :]
-
-    def tap(a, b):
-        n = 3 * (a + 1) + b + 1
-        return taps[:, n:n + 1]
-
-    lane = lax.broadcasted_iota(jnp.int32, (fb, cols), 1)
-    weight = {(a, b): jnp.broadcast_to(tap(a, b), (fb, cols)) for a in (-1, 0, 1) for b in (-1, 0, 1)}
-    first, last = lane == 0, lane == cols - 1
-    parts = {}
-    top = bottom = None
-    for r in range(rows + 1):
-        if r < rows:
-            mid = g[:, r * cols:(r + 1) * cols].astype(jnp.float32)
-            after = jnp.where(last, 0.0, pltpu.roll(mid, cols - 1, 1))
-            before = jnp.where(first, 0.0, pltpu.roll(mid, 1, 1))
-            for a in (-1, 0, 1):
-                parts[a, r] = weight[a, -1] * after + weight[a, 0] * mid + weight[a, 1] * before
-        if r == 0:
-            top = parts[-1, 0]
-        else:
-            i = r - 1
-            total = parts[0, i]
-            if i > 0:
-                total = total + parts[1, i - 1]
-            if i < rows - 1:
-                total = total + parts[-1, i + 1]
-            local_ref[part, i * cols:(i + 1) * cols] = total
-    bottom = parts[1, rows - 1]
+    shape = (taps.shape[0], cols)
+    return {(a, b): jnp.broadcast_to(taps[:, 3 * a + b + 4:3 * a + b + 5], shape)
+            for a in (-1, 0, 1) for b in (-1, 0, 1)}
+
+
+def row_part(weight, a, row):
+    after, mid, before = row
+    return weight[a, -1] * after + weight[a, 0] * mid + weight[a, 1] * before
+
+
+def interior(rows, cols, low, high, part, g_ref, k_ref, local_ref):
+    weight = taps_of(k_ref, part, cols)
+    totals = {}
+    for r in range(max(low - 1, 0), min(high + 1, rows)):
+        row = shifted(g_ref, part, r, cols)
+        for a in (-1, 0, 1):
+            i = r + a
+            if low <= i < high:
+                value = row_part(weight, a, row)
+                totals[i] = totals[i] + value if i in totals else value
+        done = r - 1
+        if done in totals:
+            local_ref[part, done * cols:(done + 1) * cols] = totals.pop(done)
+    for i, total in totals.items():
+        local_ref[part, i * cols:(i + 1) * cols] = total
+
+
+def edges(rows, cols, part, keep_top, keep_bottom,
+          g_ref, k_ref, oh_ref, sel_ref, vals_ref, top_ref, bottom_ref):
+    weight = taps_of(k_ref, part, cols)
+    top = row_part(weight, -1, shifted(g_ref, part, 0, cols))
+    bottom = row_part(weight, 1, shifted(g_ref, part, rows - 1, cols))
     top_ref[part, :] = (top * keep_top).astype(jnp.bfloat16)
     bottom_ref[part, :] = (bottom * keep_bottom).astype(jnp.bfloat16)
-    top, bottom = top.astype(jnp.bfloat16), bottom.astype(jnp.bfloat16)
-    edge = jnp.dot(g, sel_ref[...], preferred_element_type=jnp.float32)
-    near = lane < cols // 2
+    edge = jnp.dot(g_ref[part, :], sel_ref[...], preferred_element_type=jnp.float32)
+    near = lax.broadcasted_iota(jnp.int32, edge.shape, 1) < cols // 2
     sides = jnp.where(near, weight[0, -1], weight[0, 1]) * edge
     sides += jnp.where(near, weight[-1, -1], weight[-1, 1]) * pltpu.roll(edge, cols - 1, 1)
     sides += jnp.where(near, weight[1, -1], weight[1, 1]) * pltpu.roll(edge, 1, 1)
-    cycle = jnp.concatenate([top, bottom, sides.astype(jnp.bfloat16)], axis=1)
+    cycle = jnp.concatenate([x.astype(jnp.bfloat16) for x in (top, bottom, sides)], axis=1)
     vals_ref[:, part] = lax.dot_general(
         oh_ref[...], cycle, (((1,), (1,)), ((), ())), preferred_element_type=jnp.float32
     ).astype(jnp.bfloat16)

time: 130 us -> 134 us (1.031)
  Pallas kernels: 121 us -> 124 us
    pallas_call x1, Pallas kernels: 114 us -> 117 us  [mix(): pl.pallas_call(functools.partial(mix_kernel, n_tile, n_lev, chunks, rows,...]
where the time goes in v3:
time: 134 us; the launch traced here: 133 us
  Pallas kernels  124 us (93%)
  local copies, waits for them, and re-layouts  7.31 us (5%)
  other arithmetic  1.68 us (1%)
    pallas_call x1, Pallas kernels, mix(): pl.pallas_call(functools.partial(mix_kernel, n_tile, n_lev, chunks, rows,...  117 us
    unnamed x5, local copies, waits for them, and re-layouts  7.09 us
    pallas_call x1, Pallas kernels, per_device(): pl.pallas_call(functools.partial(deposit_kernel, rows, cols), grid=grid,...  6.99 us

profile of v3, /device:TPU:17, one launch (start us, length us, event | category | flops | bytes accessed | tf_op | source)
XLA Modules:
  0.0 133.4 jit_solution(15597369687572922655)
XLA Ops:
  0.0 0.8 fusion.2
  0.8 0.1 eq.34
  0.9 0.8 fusion.1
  1.7 0.1 copy.12
  1.8 0.1 reshape.14.cell_ref
  2.0 0.1 fusion.oh_ref
  2.1 1.0 copy.10.k_ref
  3.0 4.9 %copy.15 = bf16[96,8,16,128]{3,1,2,0:T(8,128)(2,1)} copy(bf16[96,8,16,128]{3,2,1,0:T(8,128)(2,1)} %bitcast.12) | data formatting | bytes 6291456
  7.9 117.3 %mix.1 = (f32[768,2048]{1,0:T(8,128)}, bf16[192,768]{1,0:T(8,128)(2,1)S(1)}, bf16[768,128]{1,0:T(8,128)(2,1)S(1)}, bf16[768,128]{1,0:T(8,128)(2,1)S(1)}, bf16[192,2048]{1,0:T(8,128)(2,1)}) custom-call(bf16[768,2048]{1,0:T(8,128)(2,1)} %bitcast.11, bf16[3072,384]{1,0:T(8,128)(2,1)} %w_ref.1, f32[768,9]{1,0:T(8,128)S(1)} %copy.10.k_ref, ...), custom_call_target="tpu_custom_call" | custom-call | tf_op jit(solution)/shard_map/mix/pallas_call | solution.py:226
  125.2 0.0 copy-start
  125.2 1.1 copy-done
  126.4 7.0 %deposit.1 = bf16[768,16,128]{2,1,0:T(8,128)(2,1)} custom-call(f32[768,2048]{1,0:T(8,128)} %get-tuple-element.10.local_ref, bf16[192,768]{1,0:T(8,128)(2,1)S(1)} %get-tuple-element.11.vals_ref, bf16[192,2048]{1,0:T(8,128)(2,1)S(1)} %copy-done, bf16[768,128]{1,0:T(8,128)(2,1)S(1)} %get-tuple-element.13.up_ref, bf16[768,128]{1,0:T(8,128)(2,1)S(1)} %get-tuple-element.14.down_ref), custom_call_target="tpu_custom_call" | custom-call | tf_op jit(solution)/shard_map/deposit/pallas_call | solution.py:368
  (3 shorter events, 0.0 us)
Async XLA Ops:
  125.2 1.1 copy-start

commit v4 on v3

--- a/solution.py
+++ b/solution.py
@@ -64,12 +64,12 @@
         copy.start()
         sends.append(copy)
 
+    for k in range(1, half_t):
+        start(w_copy(0, k, t, own_w, t_of(t, k)))
+    start(w_copy(1, 0, t, own_w, t_mate))
     for ch in range(chunks):
         for k in range(1, half_l):
             start(c_copy(0, k, ch, l, c_piece(c_ref, ch), l_of(l, k)))
-    for k in range(1, half_t):
-        start(w_copy(0, k, t, own_w, t_of(t, k)))
-    start(w_copy(1, 0, t, own_w, t_mate))
     for ch in range(chunks):
         start(c_copy(1, 0, ch, l, c_piece(c_ref, ch), l_mate))
     keep_w = pltpu.make_async_copy(own_w, w_slot(t), local_sem.at[0])
@@ -110,12 +110,8 @@
             c_copy(0, k, ch, index, c_piece(c_ref, ch), l_of(l, k)).wait_recv()
             start(c_copy(1, k, ch, index, c_piece(cg.at[index], ch), l_mate))
 
-    passed = 0
     for k in range(1, half_t):
         pass_w(k)
-        while passed < chunks - 1 and passed * (half_t - 1) < k * (chunks - 1):
-            pass_c(passed)
-            passed += 1
     keep_w.wait()
     keep_c.wait()
     for k in range(half_t):
@@ -142,8 +138,7 @@
         kept.append(copy)
 
     for ch in range(chunks):
-        if ch >= passed:
-            pass_c(ch)
+        pass_c(ch)
         for k in range(half_l):
             c_copy(1, k, ch, l_of(l_mate, -k), c_piece(c_ref, ch), l_mate).wait_recv()
 

time: 134 us -> 140 us (1.045)
  the two profiles are of different devices: /device:TPU:17 before, /device:TPU:0 now
where the time goes in v4:
time: 140 us; the launch traced here: 139 us
  Pallas kernels  130 us (93%)
  local copies, waits for them, and re-layouts  7.31 us (5%)
  other arithmetic  1.68 us (1%)
    pallas_call x1, Pallas kernels, mix(): pl.pallas_call(functools.partial(mix_kernel, n_tile, n_lev, chunks, rows,...  123 us
    unnamed x5, local copies, waits for them, and re-layouts  7.09 us
    pallas_call x1, Pallas kernels, per_device(): pl.pallas_call(functools.partial(deposit_kernel, rows, cols), grid=grid,...  6.95 us

profile of v4, /device:TPU:0, one launch (start us, length us, event | category | flops | bytes accessed | tf_op | source)
XLA Modules:
  0.0 139.4 jit_solution(9714831299013081464)
XLA Ops:
  0.0 0.8 fusion.2
  0.8 0.1 eq.34
  0.9 0.8 fusion.1
  1.7 0.1 copy.12
  1.8 0.1 reshape.14.cell_ref
  2.0 0.1 fusion.oh_ref
  2.1 1.0 copy.10.k_ref
  3.0 4.9 %copy.15 = bf16[96,8,16,128]{3,1,2,0:T(8,128)(2,1)} copy(bf16[96,8,16,128]{3,2,1,0:T(8,128)(2,1)} %bitcast.12) | data formatting | bytes 6291456
  7.9 123.3 %mix.1 = (f32[768,2048]{1,0:T(8,128)}, bf16[192,768]{1,0:T(8,128)(2,1)S(1)}, bf16[768,128]{1,0:T(8,128)(2,1)S(1)}, bf16[768,128]{1,0:T(8,128)(2,1)S(1)}, bf16[192,2048]{1,0:T(8,128)(2,1)}) custom-call(bf16[768,2048]{1,0:T(8,128)(2,1)} %bitcast.11, bf16[3072,384]{1,0:T(8,128)(2,1)} %w_ref.1, f32[768,9]{1,0:T(8,128)S(1)} %copy.10.k_ref, ...), custom_call_target="tpu_custom_call" | custom-call | tf_op jit(solution)/shard_map/mix/pallas_call | solution.py:221
  131.3 0.0 copy-start
  131.3 1.1 copy-done
  132.4 7.0 %deposit.1 = bf16[768,16,128]{2,1,0:T(8,128)(2,1)} custom-call(f32[768,2048]{1,0:T(8,128)} %get-tuple-element.10.local_ref, bf16[192,768]{1,0:T(8,128)(2,1)S(1)} %get-tuple-element.11.vals_ref, bf16[192,2048]{1,0:T(8,128)(2,1)S(1)} %copy-done, bf16[768,128]{1,0:T(8,128)(2,1)S(1)} %get-tuple-element.13.up_ref, bf16[768,128]{1,0:T(8,128)(2,1)S(1)} %get-tuple-element.14.down_ref), custom_call_target="tpu_custom_call" | custom-call | tf_op jit(solution)/shard_map/deposit/pallas_call | solution.py:363
  (3 shorter events, 0.0 us)
Async XLA Ops:
  131.3 1.1 copy-start

commit v5 on v3

--- a/solution.py
+++ b/solution.py
@@ -122,12 +122,10 @@
         w_copy(1, k, t_of(t_mate, -k), own_w, t_mate).wait_recv()
 
     rows = feat // 3
-    span = width // cols
     kept = []
 
     def run_interior(ch):
-        low = max(ch * span - 1, 0)
-        high = rows_n if ch == chunks - 1 else (ch + 1) * span - 1
+        low, high = 0, rows_n
 
         def step(m, carry):
             part = pl.ds(pl.multiple_of(m * 128, 128), 128)
@@ -166,8 +164,6 @@
             return carry
 
         lax.fori_loop(0, 3, body, 0)
-        if ch < chunks - 1:
-            run_interior(ch)
 
     strips = n_tile // 2
     q = lax.rem(t + strips // 2, n_tile)

time: 134 us -> 127 us (0.948)
  Pallas kernels: 124 us -> 117 us
    pallas_call x1, Pallas kernels: 117 us -> 110 us  [mix(): pl.pallas_call(functools.partial(mix_kernel, n_tile, n_lev, chunks, rows,...]
where the time goes in v5:
time: 127 us; the launch traced here: 126 us
  Pallas kernels  117 us (92%)
  local copies, waits for them, and re-layouts  7.31 us (6%)
  other arithmetic  1.68 us (1%)
    pallas_call x1, Pallas kernels, mix(): pl.pallas_call(functools.partial(mix_kernel, n_tile, n_lev, chunks, rows,...  110 us
    unnamed x5, local copies, waits for them, and re-layouts  7.09 us
    pallas_call x1, Pallas kernels, per_device(): pl.pallas_call(functools.partial(deposit_kernel, rows, cols), grid=grid,...  7.01 us

profile of v5, /device:TPU:17, one launch (start us, length us, event | category | flops | bytes accessed | tf_op | source)
XLA Modules:
  0.0 126.3 jit_solution(12465042530525579240)
XLA Ops:
  0.0 0.8 fusion.2
  0.8 0.1 eq.34
  0.9 0.8 fusion.1
  1.7 0.1 copy.12
  1.8 0.1 reshape.14.cell_ref
  2.0 0.1 fusion.oh_ref
  2.1 1.0 copy.10.k_ref
  3.0 4.9 %copy.15 = bf16[96,8,16,128]{3,1,2,0:T(8,128)(2,1)} copy(bf16[96,8,16,128]{3,2,1,0:T(8,128)(2,1)} %bitcast.12) | data formatting | bytes 6291456
  7.9 110.2 %mix.1 = (f32[768,2048]{1,0:T(8,128)}, bf16[192,768]{1,0:T(8,128)(2,1)S(1)}, bf16[768,128]{1,0:T(8,128)(2,1)S(1)}, bf16[768,128]{1,0:T(8,128)(2,1)S(1)}, bf16[192,2048]{1,0:T(8,128)(2,1)}) custom-call(bf16[768,2048]{1,0:T(8,128)(2,1)} %bitcast.11, bf16[3072,384]{1,0:T(8,128)(2,1)} %w_ref.1, f32[768,9]{1,0:T(8,128)S(1)} %copy.10.k_ref, ...), custom_call_target="tpu_custom_call" | custom-call | tf_op jit(solution)/shard_map/mix/pallas_call | solution.py:222
  118.1 0.0 copy-start
  118.1 1.1 copy-done
  119.3 7.0 %deposit.1 = bf16[768,16,128]{2,1,0:T(8,128)(2,1)} custom-call(f32[768,2048]{1,0:T(8,128)} %get-tuple-element.10.local_ref, bf16[192,768]{1,0:T(8,128)(2,1)S(1)} %get-tuple-element.11.vals_ref, bf16[192,2048]{1,0:T(8,128)(2,1)S(1)} %copy-done, bf16[768,128]{1,0:T(8,128)(2,1)S(1)} %get-tuple-element.13.up_ref, bf16[768,128]{1,0:T(8,128)(2,1)S(1)} %get-tuple-element.14.down_ref), custom_call_target="tpu_custom_call" | custom-call | tf_op jit(solution)/shard_map/deposit/pallas_call | solution.py:364
  (3 shorter events, 0.0 us)
Async XLA Ops:
  118.1 1.1 copy-start
